TPU v7x, 512 devices: a whole 4x4x16 slice. The times are simulated.
512 devices in a mesh: wide: 64 (over z_lo, y, core), beta: 8 (over z_hi, x).
Axes of the slice: x: 4, y: 4, z: 16 (z_hi: 2, z_lo: 8; z = z_hi * 8 + z_lo), core: 2. Of those that a mesh axis runs over, the one named last changes fastest.
Arguments:
- samples: float32 [2, 8, 1024, 1024], P(None, None, 'wide', 'beta'), may hold values from -6 to 6
- wigner: bfloat16 [8, 1024, 512, 2, 128], P(None, 'wide', 'beta'), may hold values from -0.25 to 0.25
Outputs:
- transform: float32 [2, 8, 1024, 2, 128], P(None, None, 'wide', None, 'beta')
All inputs are finite; a program needn't handle non-finite values.
Results may differ from a plain program's by a relative error of at most 0.0029.
Values may be sent and summed in bfloat16 or wider, within the bound.
A program may use at most 64 MiB of HBM per device.

v0:
```python
import math

import jax
import jax.numpy as jnp
import ml_dtypes
import numpy as np
from jax import lax
from jax.experimental import pallas as pl
from jax.experimental.pallas import tpu as pltpu
from jax.sharding import PartitionSpec as P

MESH = pl.DeviceIdType.MESH
BF16 = jnp.bfloat16
F32 = jnp.float32


def tables():
    lane = np.arange(128)
    k1, n3 = lane // 16, lane % 16
    rows = []
    for v in range(8):
        angle = 2 * math.pi * ((16 * v + n3) * k1 % 1024) / 1024
        rows.append(np.stack([np.cos(angle), -np.sin(angle)]) / 32)
    for k2 in range(8):
        angle = 2 * math.pi * (n3 * k2 % 128) / 128
        rows.append(np.stack([np.cos(angle), -np.sin(angle)]))
    twiddle = np.stack(rows).astype(np.float32)

    step = np.zeros((2, 8, 16, 2, 2, 8, 8))
    three = np.arange(16)
    for first in range(8):
        for h in range(2):
            for z in range(8):
                angle = 2 * math.pi * (three * (2 * z + h) % 16) / 16
                cosine, sine = np.cos(angle), np.sin(angle)
                step[0, first, :, h, 0, z, first] = cosine
                step[0, first, :, h, 1, z, first] = -sine
                step[1, first, :, h, 0, z, first] = sine
                step[1, first, :, h, 1, z, first] = cosine
    step = step.reshape(256, 256)
    high = step.astype(ml_dtypes.bfloat16)
    low = (step - high.astype(np.float64)).astype(ml_dtypes.bfloat16)
    step = np.concatenate([high, low])

    place = np.zeros((2, 2, 8, 2, 2, 3, 8, 2, 2, 2, 2))
    for m, part, half, low, parity in np.ndindex(2, 2, 8, 2, 2):
        place[m, part, half, low, parity, :, half, parity, low, m, part] = 1
    return twiddle, step, place.reshape(128, 384).astype(ml_dtypes.bfloat16)


def turn(value, eighths):
    re, im = value
    root = math.sqrt(0.5)
    if eighths == 0:
        return value
    if eighths == 1:
        return (re + im) * root, (im - re) * root
    if eighths == 2:
        return im, -re
    return (im - re) * root, -(re + im) * root


def butterfly(values):
    count = len(values)
    if count == 1:
        return values
    even, odd = butterfly(values[0::2]), butterfly(values[1::2])
    low, high = [], []
    for k in range(count // 2):
        a, b = even[k], turn(odd[k], k * 8 // count)
        low.append((a[0] + b[0], a[1] + b[1]))
        high.append((a[0] - b[0], a[1] - b[1]))
    return low + high


def kernel(
    samples_hbm, wigner, step_hbm, place_hbm, twiddle_hbm, out,
    samples, wig, step, place, twiddle, send_a, buf_a, send_b, buf_b, send_c, buf_c, send_d, buf_d,
    gathered, own_e, send_e, buf_e, send_f, buf_f, send_sem, recv_sem, recv_d_sem, load_sem, wigner_sem,
):
    wide, beta = lax.axis_index("wide"), lax.axis_index("beta")
    z, v = wide // 8, wide % 8
    z_hi, x = beta // 4, beta % 4
    other = (beta + 4) % 8

    load_samples = pltpu.make_async_copy(samples_hbm, samples, load_sem.at[0])
    load_twiddle = pltpu.make_async_copy(twiddle_hbm, twiddle, load_sem.at[1])
    load_step = pltpu.make_async_copy(step_hbm, step, load_sem.at[2])
    load_place = pltpu.make_async_copy(place_hbm, place, load_sem.at[3])
    load_wigner = [
        pltpu.make_async_copy(wigner.at[m], wig.at[m], wigner_sem.at[m]) for m in range(8)
    ]
    load_samples.start()

    line = [(((z + d) % 8) * 8 + v, beta) for d in range(1, 8)]
    far = [(((z + d) % 8) * 8 + v, other) for d in range(8)]
    plane = [(z * 8 + (v + d) % 8, beta) for d in range(1, 8)]
    ring = [(wide, z_hi * 4 + (x + d) % 4) for d in range(1, 4)]
    peers = far + line + plane + ring
    barrier = pltpu.get_barrier_semaphore()
    for at_wide, at_beta in peers:
        pl.semaphore_signal(
            barrier, inc=1, device_id={"wide": at_wide, "beta": at_beta}, device_id_type=MESH
        )
    for load in (load_twiddle, load_step, load_place, *load_wigner):
        load.start()

    lane = lax.broadcasted_iota(jnp.int32, (16, 128), 1)
    first = lane % 2 == 0
    load_samples.wait()
    for m in range(8):
        for side in range(2):
            cycle = 127 - lane // 2 if side else lane // 2
            re, im = [jnp.take_along_axis(samples[part, m], cycle, axis=1) for part in range(2)]
            send_a[8 * side + m] = jnp.where(first, re, im)
    pl.semaphore_wait(barrier, len(peers))

    def send(source, target, to, sent, arrived):
        pltpu.make_async_remote_copy(
            src_ref=source,
            dst_ref=target,
            send_sem=sent,
            recv_sem=arrived,
            device_id={"wide": to[0], "beta": to[1]},
            device_id_type=MESH,
        ).start()

    def wait(block, semaphore):
        pltpu.make_async_copy(block, block, semaphore).wait()

    pltpu.make_async_copy(send_a.at[z], buf_a.at[z], recv_sem.at[0]).start()
    send(send_a.at[8 + z], buf_a.at[8 + z], far[0], send_sem.at[0], recv_sem.at[0])
    for to_hi in (1, 0):
        side = 1 - z_hi if to_hi else z_hi
        for d in range(1, 8):
            to = (z + d) % 8
            send(
                send_a.at[8 * side + to],
                buf_a.at[8 * side + z],
                (8 * to + v, 4 * to_hi + x),
                send_sem.at[0],
                recv_sem.at[0],
            )
    load_twiddle.wait()
    wait(buf_a, recv_sem.at[0])
    sign = (1 - 2 * z_hi).astype(F32)
    values = []
    for n in range(8):
        own, mirror = buf_a[n], buf_a[8 + n]
        even, odd = own + mirror, (own - mirror) * sign
        re = jnp.where(first, even, pltpu.roll(odd, 1, 1))
        im = jnp.where(first, pltpu.roll(even, 127, 1), odd)
        values.append((re, im))
    done = butterfly(values)
    re = jnp.concatenate([value[0] for value in done], axis=0).T
    im = jnp.concatenate([value[1] for value in done], axis=0).T
    factor = twiddle[v]
    cosine, sine = factor[0:1], factor[1:2]
    send_b[:, 0] = (re * cosine - im * sine).reshape(8, 16, 128)
    send_b[:, 1] = (re * sine + im * cosine).reshape(8, 16, 128)

    pltpu.make_async_copy(send_b.at[v], buf_b.at[v], recv_sem.at[1]).start()
    for d in range(1, 8):
        source, target = send_b.at[(v + d) % 8], buf_b.at[v]
        send(source, target, plane[d - 1], send_sem.at[1], recv_sem.at[1])
    wait(send_a.at[pl.ds(0, 15)], send_sem.at[0])
    load_step.wait()
    load_place.wait()
    wait(buf_b, recv_sem.at[1])
    done = butterfly([(buf_b[n, 0], buf_b[n, 1]) for n in range(8)])
    turned = []
    for k2 in range(8):
        re, im = done[k2]
        factor = twiddle[8 + k2]
        cosine, sine = factor[0:1], factor[1:2]
        turned.append(
            jnp.concatenate([re * cosine - im * sine, re * sine + im * cosine], axis=1)
        )
    values = jnp.concatenate(turned[0::2] + turned[1::2], axis=0)
    high = values.astype(BF16)
    low = (values - high.astype(F32)).astype(BF16)
    both = jnp.concatenate([high, low], axis=0)
    main = jnp.dot(both, step[0:256], preferred_element_type=F32)
    rest = jnp.dot(high, step[256:512], preferred_element_type=F32)
    spectrum = main[0:128] + (main[128:256] + rest)
    first_half = lax.broadcasted_iota(jnp.int32, (64, 128), 1) < 64
    for h in range(2):
        a = spectrum[0:64, 128 * h : 128 * h + 128]
        b = spectrum[64:128, 128 * h : 128 * h + 128]
        re = jnp.where(first_half, a, pltpu.roll(b, 64, 1))
        im = jnp.where(first_half, pltpu.roll(a, 64, 1), b)
        send_c[4 * h : 4 * h + 4, 0] = re.astype(BF16).reshape(4, 16, 128)
        send_c[4 * h : 4 * h + 4, 1] = im.astype(BF16).reshape(4, 16, 128)

    pltpu.make_async_copy(send_c.at[v], buf_c.at[v], recv_sem.at[2]).start()
    for d in range(1, 8):
        source, target = send_c.at[(v + d) % 8], buf_c.at[v]
        send(source, target, plane[d - 1], send_sem.at[2], recv_sem.at[2])
    wait(send_b.at[pl.ds(0, 7)], send_sem.at[1])
    wait(buf_c, recv_sem.at[2])
    for part in range(2):
        values = buf_c[:, part].reshape(128, 128).astype(F32).T
        values = [values[64 * e : 64 * e + 64].reshape(8, 8, 128) for e in range(2)]
        send_d[:, part] = jnp.concatenate(values, axis=1).astype(BF16)

    pltpu.make_async_copy(send_d.at[z], buf_d.at[z], recv_d_sem.at[0]).start()
    for d in range(1, 8):
        source, target = send_d.at[(z + d) % 8], buf_d.at[z]
        send(source, target, line[d - 1], send_sem.at[3], recv_d_sem.at[d])
    wait(send_c.at[pl.ds(0, 7)], send_sem.at[2])

    row = lax.broadcasted_iota(jnp.int32, (8, 128), 0)
    lane = lax.broadcasted_iota(jnp.int32, (8, 128), 1)
    fits = [[(lane % 2 == parity) & (row // 4 == low) for low in range(2)] for parity in range(2)]
    second = lax.broadcasted_iota(jnp.int32, (16, 128), 0) // 2 % 2 == 1

    def products(g):
        steps = (2 * g, 2 * g + 1)
        orders = [(z + 8 - d) % 8 for d in steps]
        for d, m in zip(steps, orders):
            wait(buf_d.at[m], recv_d_sem.at[d])
        for at, m in enumerate(orders):
            pltpu.make_async_copy(wigner.at[m], wig.at[m], wigner_sem.at[m]).wait()
            for part in range(2):
                gathered[g, pl.ds(2 * at + part, 16, stride=4)] = buf_d[m, part].astype(F32)
        terms = []
        for i in range(8):
            rows = gathered[g, 8 * i : 8 * i + 8]
            pairs = [
                jnp.concatenate([jnp.where(fit, rows, 0.0) for fit in parity], axis=1)
                for parity in fits
            ]
            weights = [wig[m, 256 * i : 256 * i + 256] for m in orders]
            both = jnp.dot(
                jnp.concatenate(pairs, axis=0).astype(BF16),
                jnp.concatenate(weights, axis=1),
                preferred_element_type=F32,
            )
            terms.append(jnp.where(second, both[:, 128:256], both[:, 0:128]))
        terms = jnp.concatenate(terms, axis=0).T
        own_e[:, g] = terms.reshape(8, 16, 128)
        terms = terms.astype(BF16)
        for owner in range(8):
            send_e[owner // 4, owner % 4, g] = terms[16 * owner : 16 * owner + 16]

    def total_of(owner):
        total = own_e[owner * 4 + x]
        for d in range(3):
            total += buf_e[owner, d].astype(F32)
        return total

    for g in range(4):
        products(g)

    for step, owner in ((4, 1 - z_hi), (5, z_hi)):
        for d in range(1, 4):
            source, target = send_e.at[owner, (x + d) % 4], buf_e.at[owner, d - 1]
            send(source, target, ring[d - 1], send_sem.at[step], recv_sem.at[step - 1])
    wait(send_d.at[pl.ds(0, 7)], send_sem.at[3])
    wait(buf_e.at[0], recv_sem.at[3])

    send_f[...] = total_of(1 - z_hi).astype(BF16)
    send(send_f, buf_f, far[0], send_sem.at[6], recv_sem.at[5])
    wait(buf_e.at[1], recv_sem.at[4])
    mine = total_of(z_hi)
    for step in (4, 5):
        wait(send_e.at[0, pl.ds(0, 3)], send_sem.at[step])
    wait(buf_f, recv_sem.at[5])
    total = mine + buf_f[...].astype(F32)
    high = total.astype(BF16)
    left = total - high.astype(F32)
    middle = left.astype(BF16)
    low = (left - middle.astype(F32)).astype(BF16)
    total = jnp.concatenate([high, middle, low], axis=2)
    row = lax.broadcasted_iota(jnp.int32, (128, 128), 0)
    lane = lax.broadcasted_iota(jnp.int32, (128, 128), 1)
    for g in range(4):
        rows = lax.dot_general(
            place[...],
            jnp.concatenate([total[g]] * 8, axis=0),
            (((1,), (1,)), ((), ())),
            preferred_element_type=F32,
        )
        rows = jnp.where(lane // 16 == row % 8, rows, 0.0).reshape(16, 8, 128).sum(axis=1)
        for at in range(2):
            for part in range(2):
                first_row = 8 * at + 4 * part
                out[part, (z + 8 - 2 * g - at) % 8] = rows[first_row : first_row + 4]
    wait(send_f, send_sem.at[6])


def body(samples, wigner):
    twiddle, step, place = tables()
    anywhere = pl.BlockSpec(memory_space=pl.ANY)
    terms = pl.pallas_call(
        kernel,
        out_shape=jax.ShapeDtypeStruct((2, 8, 4, 128), F32),
        in_specs=[anywhere] * 5,
        out_specs=pl.BlockSpec(memory_space=pltpu.VMEM),
        scratch_shapes=[
            pltpu.VMEM((2, 8, 16, 128), F32),
            pltpu.VMEM((8, 2048, 128), BF16),
            pltpu.VMEM((512, 256), BF16),
            pltpu.VMEM((128, 384), BF16),
            pltpu.VMEM((16, 2, 128), F32),
            pltpu.VMEM((16, 16, 128), F32),
            pltpu.VMEM((16, 16, 128), F32),
            pltpu.VMEM((8, 2, 16, 128), F32),
            pltpu.VMEM((8, 2, 16, 128), F32),
            pltpu.VMEM((8, 2, 16, 128), BF16),
            pltpu.VMEM((8, 2, 16, 128), BF16),
            pltpu.VMEM((8, 2, 16, 128), BF16),
            pltpu.VMEM((8, 2, 16, 128), BF16),
            pltpu.VMEM((4, 64, 128), F32),
            pltpu.VMEM((8, 4, 16, 128), F32),
            pltpu.VMEM((2, 4, 4, 16, 128), BF16),
            pltpu.VMEM((2, 3, 4, 16, 128), BF16),
            pltpu.VMEM((4, 16, 128), BF16),
            pltpu.VMEM((4, 16, 128), BF16),
            pltpu.SemaphoreType.DMA((7,)),
            pltpu.SemaphoreType.DMA((6,)),
            pltpu.SemaphoreType.DMA((8,)),
            pltpu.SemaphoreType.DMA((4,)),
            pltpu.SemaphoreType.DMA((8,)),
        ],
        compiler_params=pltpu.CompilerParams(
            collective_id=0, has_side_effects=True, vmem_limit_bytes=60 * 1024 * 1024
        ),
    )(
        samples,
        wigner.reshape(8, 2048, 128),
        jnp.asarray(step),
        jnp.asarray(place),
        jnp.asarray(twiddle),
    )
    return terms.reshape(2, 8, 16, 2, 16)


def solution(mesh):
    return jax.shard_map(
        body,
        mesh=mesh,
        in_specs=(P(None, None, "wide", "beta"), P(None, "wide", "beta", None, None)),
        out_specs=P(None, None, "wide", None, "beta"),
        check_vma=False,
    )
```

profile of v0, /device:TPU:24, one launch (start us, length us, event | category | flops | bytes accessed | tf_op | source)
XLA Modules:
  0.0 53.8 jit_solution(16256903907722724579)
XLA Ops:
  0.0 51.9 %shard_map.55 = f32[2,8,4,128]{3,2,1,0:T(4,128)} custom-call(f32[2,8,16,128]{3,2,1,0:T(8,128)} %samples_hbm.1, bf16[8,2048,128]{2,1,0:T(8,128)(2,1)} %bitcast.1, bf16[512,256]{1,0:T(8,128)(2,1)} %constant.6.clone.step_hbm, bf16[128,384]{1,0:T(8,128)(2,1)} %constant.7.clone.place_hbm, f32[16,2,128]{2,1,0:T(2,128)} %constant.8.clone.twiddle_hbm), custom_call_target="tpu_custom_call" | custom-call | tf_op jit(solution)/shard_map/pallas_call | solution.py:295
  51.9 1.8 %reshape.7 = f32[2,8,16,2,16]{4,3,2,1,0:T(2,128)} reshape(f32[2,8,4,128]{3,2,1,0:T(4,128)} %shard_map.55) | data formatting | bytes 65536 | tf_op jit(solution)/shard_map/reshape | solution.py:336
where the time goes:
time: 54.2 us; the launch traced here: 53.8 us
  Pallas kernels  51.9 us (96%)
  local copies, waits for them, and re-layouts  1.84 us (3%)
    pallas_call x1, Pallas kernels, body(): pl.pallas_call(kernel, out_shape=jax.ShapeDtypeStruct((2, 8, 4, 128), F32...  51.9 us
    reshape x1, local copies, waits for them, and re-layouts, body(): return terms.reshape(2, 8, 16, 2, 16)  1.84 us

commit v1 on v0

--- a/solution.py
+++ b/solution.py
@@ -92,11 +92,14 @@
     ]
     load_samples.start()
 
-    line = [(((z + d) % 8) * 8 + v, beta) for d in range(1, 8)]
-    far = [(((z + d) % 8) * 8 + v, other) for d in range(8)]
+    def across(d):
+        return sum((z // bit + d // bit) % 2 * bit for bit in (1, 2, 4))
+
+    line = [(across(d) * 8 + v, beta) for d in range(1, 8)]
+    far = [(across(d) * 8 + v, other) for d in range(8)]
     plane = [(z * 8 + (v + d) % 8, beta) for d in range(1, 8)]
     ring = [(wide, z_hi * 4 + (x + d) % 4) for d in range(1, 4)]
-    peers = far + line + plane + ring
+    peers = far + line[::-1] + plane + ring
     barrier = pltpu.get_barrier_semaphore()
     for at_wide, at_beta in peers:
         pl.semaphore_signal(
@@ -132,8 +135,8 @@
     send(send_a.at[8 + z], buf_a.at[8 + z], far[0], send_sem.at[0], recv_sem.at[0])
     for to_hi in (1, 0):
         side = 1 - z_hi if to_hi else z_hi
-        for d in range(1, 8):
-            to = (z + d) % 8
+        for k in range(1, 8):
+            to = across(8 - k + side * (2 * k - 8))
             send(
                 send_a.at[8 * side + to],
                 buf_a.at[8 * side + z],
@@ -160,7 +163,7 @@
     send_b[:, 1] = (re * sine + im * cosine).reshape(8, 16, 128)
 
     pltpu.make_async_copy(send_b.at[v], buf_b.at[v], recv_sem.at[1]).start()
-    for d in range(1, 8):
+    for d in (4, 3, 5, 2, 6, 1, 7):
         source, target = send_b.at[(v + d) % 8], buf_b.at[v]
         send(source, target, plane[d - 1], send_sem.at[1], recv_sem.at[1])
     wait(send_a.at[pl.ds(0, 15)], send_sem.at[0])
@@ -193,7 +196,7 @@
         send_c[4 * h : 4 * h + 4, 1] = im.astype(BF16).reshape(4, 16, 128)
 
     pltpu.make_async_copy(send_c.at[v], buf_c.at[v], recv_sem.at[2]).start()
-    for d in range(1, 8):
+    for d in (4, 3, 5, 2, 6, 1, 7):
         source, target = send_c.at[(v + d) % 8], buf_c.at[v]
         send(source, target, plane[d - 1], send_sem.at[2], recv_sem.at[2])
     wait(send_b.at[pl.ds(0, 7)], send_sem.at[1])
@@ -204,8 +207,8 @@
         send_d[:, part] = jnp.concatenate(values, axis=1).astype(BF16)
 
     pltpu.make_async_copy(send_d.at[z], buf_d.at[z], recv_d_sem.at[0]).start()
-    for d in range(1, 8):
-        source, target = send_d.at[(z + d) % 8], buf_d.at[z]
+    for d in range(7, 0, -1):
+        source, target = send_d.at[across(d)], buf_d.at[z]
         send(source, target, line[d - 1], send_sem.at[3], recv_d_sem.at[d])
     wait(send_c.at[pl.ds(0, 7)], send_sem.at[2])
 
@@ -216,7 +219,7 @@
 
     def products(g):
         steps = (2 * g, 2 * g + 1)
-        orders = [(z + 8 - d) % 8 for d in steps]
+        orders = [across(d) for d in steps]
         for d, m in zip(steps, orders):
             wait(buf_d.at[m], recv_d_sem.at[d])
         for at, m in enumerate(orders):
@@ -253,7 +256,7 @@
         products(g)
 
     for step, owner in ((4, 1 - z_hi), (5, z_hi)):
-        for d in range(1, 4):
+        for d in (2, 1, 3):
             source, target = send_e.at[owner, (x + d) % 4], buf_e.at[owner, d - 1]
             send(source, target, ring[d - 1], send_sem.at[step], recv_sem.at[step - 1])
     wait(send_d.at[pl.ds(0, 7)], send_sem.at[3])
@@ -285,7 +288,7 @@
         for at in range(2):
             for part in range(2):
                 first_row = 8 * at + 4 * part
-                out[part, (z + 8 - 2 * g - at) % 8] = rows[first_row : first_row + 4]
+                out[part, across(2 * g + at)] = rows[first_row : first_row + 4]
     wait(send_f, send_sem.at[6])
 
 

time: 54.2 us -> 53.6 us (0.989)
    pallas_call x1, Pallas kernels: 51.9 us -> 51.4 us  [body(): pl.pallas_call(kernel, out_shape=jax.ShapeDtypeStruct((2, 8, 4, 128), F32...]
where the time goes in v1:
time: 53.6 us; the launch traced here: 53.2 us
  Pallas kernels  51.4 us (96%)
  local copies, waits for them, and re-layouts  1.84 us (3%)
    pallas_call x1, Pallas kernels, body(): pl.pallas_call(kernel, out_shape=jax.ShapeDtypeStruct((2, 8, 4, 128), F32...  51.4 us
    reshape x1, local copies, waits for them, and re-layouts, body(): return terms.reshape(2, 8, 16, 2, 16)  1.84 us

profile of v1, /device:TPU:24, one launch (start us, length us, event | category | flops | bytes accessed | tf_op | source)
XLA Modules:
  0.0 53.2 jit_solution(5723780038406442255)
XLA Ops:
  0.0 51.4 %shard_map.55 = f32[2,8,4,128]{3,2,1,0:T(4,128)} custom-call(f32[2,8,16,128]{3,2,1,0:T(8,128)} %samples_hbm.1, bf16[8,2048,128]{2,1,0:T(8,128)(2,1)} %bitcast.1, bf16[512,256]{1,0:T(8,128)(2,1)} %constant.6.clone.step_hbm, bf16[128,384]{1,0:T(8,128)(2,1)} %constant.7.clone.place_hbm, f32[16,2,128]{2,1,0:T(2,128)} %constant.8.clone.twiddle_hbm), custom_call_target="tpu_custom_call" | custom-call | tf_op jit(solution)/shard_map/pallas_call | solution.py:298
  51.4 1.8 %reshape.7 = f32[2,8,16,2,16]{4,3,2,1,0:T(2,128)} reshape(f32[2,8,4,128]{3,2,1,0:T(4,128)} %shard_map.55) | data formatting | bytes 65536 | tf_op jit(solution)/shard_map/reshape | solution.py:339

commit v2 on v1

--- a/solution.py
+++ b/solution.py
@@ -75,7 +75,7 @@
 
 def kernel(
     samples_hbm, wigner, step_hbm, place_hbm, twiddle_hbm, out,
-    samples, wig, step, place, twiddle, send_a, buf_a, send_b, buf_b, send_c, buf_c, send_d, buf_d,
+    samples, wig, step, place, twiddle, send_a, buf_a, send_m, buf_m, send_b, buf_b, send_c, buf_c, send_d, buf_d,
     gathered, own_e, send_e, buf_e, send_f, buf_f, send_sem, recv_sem, recv_d_sem, load_sem, wigner_sem,
 ):
     wide, beta = lax.axis_index("wide"), lax.axis_index("beta")
@@ -116,6 +116,8 @@
             cycle = 127 - lane // 2 if side else lane // 2
             re, im = [jnp.take_along_axis(samples[part, m], cycle, axis=1) for part in range(2)]
             send_a[8 * side + m] = jnp.where(first, re, im)
+            if side:
+                send_m[m] = jnp.where(first, re, im).astype(BF16)
     pl.semaphore_wait(barrier, len(peers))
 
     def send(source, target, to, sent, arrived):
@@ -132,20 +134,39 @@
         pltpu.make_async_copy(block, block, semaphore).wait()
 
     pltpu.make_async_copy(send_a.at[z], buf_a.at[z], recv_sem.at[0]).start()
-    send(send_a.at[8 + z], buf_a.at[8 + z], far[0], send_sem.at[0], recv_sem.at[0])
-    for to_hi in (1, 0):
-        side = 1 - z_hi if to_hi else z_hi
-        for k in range(1, 8):
-            to = across(8 - k + side * (2 * k - 8))
-            send(
-                send_a.at[8 * side + to],
-                buf_a.at[8 * side + z],
-                (8 * to + v, 4 * to_hi + x),
-                send_sem.at[0],
-                recv_sem.at[0],
-            )
+
+    def send_own():
+        for d in range(7, 0, -1):
+            source, target = send_a.at[across(d)], buf_a.at[z]
+            send(source, target, line[d - 1], send_sem.at[0], recv_sem.at[0])
+
+    @pl.when(z_hi == 0)
+    def _():
+        for d in range(8):
+            source, target = send_m.at[across(d)], buf_m.at[z]
+            send(source, target, far[d], send_sem.at[7], recv_sem.at[6])
+        send_own()
+
+    @pl.when(z_hi == 1)
+    def _():
+        send_own()
+        for d in range(8):
+            source, target = send_a.at[8 + across(d)], buf_a.at[8 + z]
+            send(source, target, far[d], send_sem.at[7], recv_sem.at[6])
+
     load_twiddle.wait()
-    wait(buf_a, recv_sem.at[0])
+    wait(buf_a.at[pl.ds(0, 8)], recv_sem.at[0])
+
+    @pl.when(z_hi == 0)
+    def _():
+        wait(buf_a.at[pl.ds(8, 8)], recv_sem.at[6])
+
+    @pl.when(z_hi == 1)
+    def _():
+        wait(buf_m, recv_sem.at[6])
+        for n in range(8):
+            buf_a[8 + n] = buf_m[n].astype(F32)
+
     sign = (1 - 2 * z_hi).astype(F32)
     values = []
     for n in range(8):
@@ -166,7 +187,16 @@
     for d in (4, 3, 5, 2, 6, 1, 7):
         source, target = send_b.at[(v + d) % 8], buf_b.at[v]
         send(source, target, plane[d - 1], send_sem.at[1], recv_sem.at[1])
-    wait(send_a.at[pl.ds(0, 15)], send_sem.at[0])
+    wait(send_a.at[pl.ds(0, 7)], send_sem.at[0])
+
+    @pl.when(z_hi == 0)
+    def _():
+        wait(send_m, send_sem.at[7])
+
+    @pl.when(z_hi == 1)
+    def _():
+        wait(send_a.at[pl.ds(8, 8)], send_sem.at[7])
+
     load_step.wait()
     load_place.wait()
     wait(buf_b, recv_sem.at[1])
@@ -308,6 +338,8 @@
             pltpu.VMEM((16, 2, 128), F32),
             pltpu.VMEM((16, 16, 128), F32),
             pltpu.VMEM((16, 16, 128), F32),
+            pltpu.VMEM((8, 16, 128), BF16),
+            pltpu.VMEM((8, 16, 128), BF16),
             pltpu.VMEM((8, 2, 16, 128), F32),
             pltpu.VMEM((8, 2, 16, 128), F32),
             pltpu.VMEM((8, 2, 16, 128), BF16),
@@ -320,8 +352,8 @@
             pltpu.VMEM((2, 3, 4, 16, 128), BF16),
             pltpu.VMEM((4, 16, 128), BF16),
             pltpu.VMEM((4, 16, 128), BF16),
+            pltpu.SemaphoreType.DMA((8,)),
             pltpu.SemaphoreType.DMA((7,)),
-            pltpu.SemaphoreType.DMA((6,)),
             pltpu.SemaphoreType.DMA((8,)),
             pltpu.SemaphoreType.DMA((4,)),
             pltpu.SemaphoreType.DMA((8,)),

time: 53.6 us -> 51.9 us (0.968)
  Pallas kernels: 51.4 us -> 49.4 us
    pallas_call x1, Pallas kernels: 51.4 us -> 49.4 us  [body(): pl.pallas_call(kernel, out_shape=jax.ShapeDtypeStruct((2, 8, 4, 128), F32...]
where the time goes in v2:
time: 51.9 us; the launch traced here: 51.2 us
  Pallas kernels  49.4 us (95%)
  local copies, waits for them, and re-layouts  1.84 us (4%)
    pallas_call x1, Pallas kernels, body(): pl.pallas_call(kernel, out_shape=jax.ShapeDtypeStruct((2, 8, 4, 128), F32...  49.4 us
    reshape x1, local copies, waits for them, and re-layouts, body(): return terms.reshape(2, 8, 16, 2, 16)  1.84 us

profile of v2, /device:TPU:24, one launch (start us, length us, event | category | flops | bytes accessed | tf_op | source)
XLA Modules:
  0.0 51.2 jit_solution(4794483232047520449)
XLA Ops:
  0.0 49.4 %shard_map.55 = f32[2,8,4,128]{3,2,1,0:T(4,128)} custom-call(f32[2,8,16,128]{3,2,1,0:T(8,128)} %samples_hbm.1, bf16[8,2048,128]{2,1,0:T(8,128)(2,1)} %bitcast.1, bf16[512,256]{1,0:T(8,128)(2,1)} %constant.6.clone.step_hbm, bf16[128,384]{1,0:T(8,128)(2,1)} %constant.7.clone.place_hbm, f32[16,2,128]{2,1,0:T(2,128)} %constant.8.clone.twiddle_hbm), custom_call_target="tpu_custom_call" | custom-call | tf_op jit(solution)/shard_map/pallas_call | solution.py:328
  49.4 1.8 %reshape.7 = f32[2,8,16,2,16]{4,3,2,1,0:T(2,128)} reshape(f32[2,8,4,128]{3,2,1,0:T(4,128)} %shard_map.55) | data formatting | bytes 65536 | tf_op jit(solution)/shard_map/reshape | solution.py:371

commit v3 on v2

--- a/solution.py
+++ b/solution.py
@@ -116,8 +116,7 @@
             cycle = 127 - lane // 2 if side else lane // 2
             re, im = [jnp.take_along_axis(samples[part, m], cycle, axis=1) for part in range(2)]
             send_a[8 * side + m] = jnp.where(first, re, im)
-            if side:
-                send_m[m] = jnp.where(first, re, im).astype(BF16)
+            send_m[8 * side + m] = jnp.where(first, re, im).astype(BF16)
     pl.semaphore_wait(barrier, len(peers))
 
     def send(source, target, to, sent, arrived):
@@ -133,39 +132,40 @@
     def wait(block, semaphore):
         pltpu.make_async_copy(block, block, semaphore).wait()
 
-    pltpu.make_async_copy(send_a.at[z], buf_a.at[z], recv_sem.at[0]).start()
-
-    def send_own():
+    def send_own(sources, targets):
+        pltpu.make_async_copy(sources.at[z], targets.at[z], recv_sem.at[0]).start()
         for d in range(7, 0, -1):
-            source, target = send_a.at[across(d)], buf_a.at[z]
+            source, target = sources.at[across(d)], targets.at[z]
             send(source, target, line[d - 1], send_sem.at[0], recv_sem.at[0])
 
+    def send_mirror(sources, targets):
+        for d in range(8):
+            source, target = sources.at[8 + across(d)], targets.at[8 + z]
+            send(source, target, far[d], send_sem.at[7], recv_sem.at[6])
+
     @pl.when(z_hi == 0)
     def _():
-        for d in range(8):
-            source, target = send_m.at[across(d)], buf_m.at[z]
-            send(source, target, far[d], send_sem.at[7], recv_sem.at[6])
-        send_own()
+        send_mirror(send_m, buf_m)
+        send_own(send_a, buf_a)
 
     @pl.when(z_hi == 1)
     def _():
-        send_own()
-        for d in range(8):
-            source, target = send_a.at[8 + across(d)], buf_a.at[8 + z]
-            send(source, target, far[d], send_sem.at[7], recv_sem.at[6])
+        send_own(send_m, buf_m)
+        send_mirror(send_a, buf_a)
 
     load_twiddle.wait()
-    wait(buf_a.at[pl.ds(0, 8)], recv_sem.at[0])
 
     @pl.when(z_hi == 0)
     def _():
+        wait(buf_a.at[pl.ds(0, 8)], recv_sem.at[0])
         wait(buf_a.at[pl.ds(8, 8)], recv_sem.at[6])
 
     @pl.when(z_hi == 1)
     def _():
-        wait(buf_m, recv_sem.at[6])
-        for n in range(8):
-            buf_a[8 + n] = buf_m[n].astype(F32)
+        wait(buf_m.at[pl.ds(0, 8)], recv_sem.at[0])
+        wait(buf_m.at[pl.ds(8, 8)], recv_sem.at[6])
+        for n in range(16):
+            buf_a[n] = buf_m[n].astype(F32)
 
     sign = (1 - 2 * z_hi).astype(F32)
     values = []
@@ -187,14 +187,15 @@
     for d in (4, 3, 5, 2, 6, 1, 7):
         source, target = send_b.at[(v + d) % 8], buf_b.at[v]
         send(source, target, plane[d - 1], send_sem.at[1], recv_sem.at[1])
-    wait(send_a.at[pl.ds(0, 7)], send_sem.at[0])
 
     @pl.when(z_hi == 0)
     def _():
-        wait(send_m, send_sem.at[7])
+        wait(send_a.at[pl.ds(0, 7)], send_sem.at[0])
+        wait(send_m.at[pl.ds(8, 8)], send_sem.at[7])
 
     @pl.when(z_hi == 1)
     def _():
+        wait(send_m.at[pl.ds(0, 7)], send_sem.at[0])
         wait(send_a.at[pl.ds(8, 8)], send_sem.at[7])
 
     load_step.wait()
@@ -338,8 +339,8 @@
             pltpu.VMEM((16, 2, 128), F32),
             pltpu.VMEM((16, 16, 128), F32),
             pltpu.VMEM((16, 16, 128), F32),
-            pltpu.VMEM((8, 16, 128), BF16),
-            pltpu.VMEM((8, 16, 128), BF16),
+            pltpu.VMEM((16, 16, 128), BF16),
+            pltpu.VMEM((16, 16, 128), BF16),
             pltpu.VMEM((8, 2, 16, 128), F32),
             pltpu.VMEM((8, 2, 16, 128), F32),
             pltpu.VMEM((8, 2, 16, 128), BF16),

time: 51.9 us -> 51.8 us (level)
  no operation moved by 1% of the time
where the time goes in v3:
time: 51.8 us; the launch traced here: 51.4 us
  Pallas kernels  49.6 us (96%)
  local copies, waits for them, and re-layouts  1.84 us (4%)
    pallas_call x1, Pallas kernels, body(): pl.pallas_call(kernel, out_shape=jax.ShapeDtypeStruct((2, 8, 4, 128), F32...  49.6 us
    reshape x1, local copies, waits for them, and re-layouts, body(): return terms.reshape(2, 8, 16, 2, 16)  1.84 us

profile of v3, /device:TPU:24, one launch (start us, length us, event | category | flops | bytes accessed | tf_op | source)
XLA Modules:
  0.0 51.4 jit_solution(15908032494114862215)
XLA Ops:
  0.0 49.6 %shard_map.55 = f32[2,8,4,128]{3,2,1,0:T(4,128)} custom-call(f32[2,8,16,128]{3,2,1,0:T(8,128)} %samples_hbm.1, bf16[8,2048,128]{2,1,0:T(8,128)(2,1)} %bitcast.1, bf16[512,256]{1,0:T(8,128)(2,1)} %constant.6.clone.step_hbm, bf16[128,384]{1,0:T(8,128)(2,1)} %constant.7.clone.place_hbm, f32[16,2,128]{2,1,0:T(2,128)} %constant.8.clone.twiddle_hbm), custom_call_target="tpu_custom_call" | custom-call | tf_op jit(solution)/shard_map/pallas_call | solution.py:329
  49.6 1.8 %reshape.7 = f32[2,8,16,2,16]{4,3,2,1,0:T(2,128)} reshape(f32[2,8,4,128]{3,2,1,0:T(4,128)} %shard_map.55) | data formatting | bytes 65536 | tf_op jit(solution)/shard_map/reshape | solution.py:372

commit v4 on v2

--- a/solution.py
+++ b/solution.py
@@ -237,7 +237,7 @@
         send_d[:, part] = jnp.concatenate(values, axis=1).astype(BF16)
 
     pltpu.make_async_copy(send_d.at[z], buf_d.at[z], recv_d_sem.at[0]).start()
-    for d in range(7, 0, -1):
+    for d in range(1, 8):
         source, target = send_d.at[across(d)], buf_d.at[z]
         send(source, target, line[d - 1], send_sem.at[3], recv_d_sem.at[d])
     wait(send_c.at[pl.ds(0, 7)], send_sem.at[2])

time: 51.9 us -> 52.3 us (level)
  Pallas kernels: 49.4 us -> 50 us
    pallas_call x1, Pallas kernels: 49.4 us -> 50 us  [body(): pl.pallas_call(kernel, out_shape=jax.ShapeDtypeStruct((2, 8, 4, 128), F32...]
where the time goes in v4:
time: 52.3 us; the launch traced here: 51.9 us
  Pallas kernels  50 us (96%)
  local copies, waits for them, and re-layouts  1.84 us (4%)
    pallas_call x1, Pallas kernels, body(): pl.pallas_call(kernel, out_shape=jax.ShapeDtypeStruct((2, 8, 4, 128), F32...  50 us
    reshape x1, local copies, waits for them, and re-layouts, body(): return terms.reshape(2, 8, 16, 2, 16)  1.84 us

profile of v4, /device:TPU:24, one launch (start us, length us, event | category | flops | bytes accessed | tf_op | source)
XLA Modules:
  0.0 51.9 jit_solution(18002706973435461332)
XLA Ops:
  0.0 50.0 %shard_map.55 = f32[2,8,4,128]{3,2,1,0:T(4,128)} custom-call(f32[2,8,16,128]{3,2,1,0:T(8,128)} %samples_hbm.1, bf16[8,2048,128]{2,1,0:T(8,128)(2,1)} %bitcast.1, bf16[512,256]{1,0:T(8,128)(2,1)} %constant.6.clone.step_hbm, bf16[128,384]{1,0:T(8,128)(2,1)} %constant.7.clone.place_hbm, f32[16,2,128]{2,1,0:T(2,128)} %constant.8.clone.twiddle_hbm), custom_call_target="tpu_custom_call" | custom-call | tf_op jit(solution)/shard_map/pallas_call | solution.py:328
  50.0 1.8 %reshape.7 = f32[2,8,16,2,16]{4,3,2,1,0:T(2,128)} reshape(f32[2,8,4,128]{3,2,1,0:T(4,128)} %shard_map.55) | data formatting | bytes 65536 | tf_op jit(solution)/shard_map/reshape | solution.py:371
